TPU v7x, 512 devices: a whole 4x8x8 slice. The times are simulated.
512 devices in a mesh: row: 16 (over z, core), col: 32 (over y, x).
Axes of the slice: x: 4, y: 8, z: 8, core: 2. Of those that a mesh axis runs over, the one named last changes fastest.
Arguments:
- train_embed: bfloat16 [8192, 256], P(('row', 'col')), may hold values from -16 to 16
- valid_embed: bfloat16 [65536, 256], P(('row', 'col')), may hold values from -16 to 16
- train_labels: int32 [8192], P(('row', 'col')), may hold values from 0 to 99
- valid_labels: int32 [65536], P(('row', 'col')), may hold values from 0 to 99
- pair_level: int32 [100, 100], replicated, may hold values from 0 to 3
- level_cost: float32 [4], replicated, may hold values from 0.05 to 1
Outputs:
- calibrated: float32 [8192], P('row')
All inputs are finite; a program needn't handle non-finite values.
Results may differ from a plain program's by a relative error of at most 0.0003.
Values may be sent and summed in bfloat16 or wider, within the bound.
No kernel may reach another device: no remote copies, remote signals or barrier semaphores. Data moves between devices by JAX's collectives and lax.ppermute only.
A program may use at most 64 MiB of HBM per device.

v0:
```python
import math
import jax
import jax.numpy as jnp
from jax import lax
from jax.sharding import PartitionSpec as P

ITERS = 4
entropy_scale = 0.05


def inner_products(left_rows, right_rows):
    return lax.dot_general(
        left_rows, right_rows, (((1,), (1,)), ((), ())), preferred_element_type=jnp.float32
    )


def squared_norms(embeddings):
    widened = embeddings.astype(jnp.float32)
    return jnp.sum(widened * widened, axis=1)


def class_costs(pair_level, level_cost):
    num_levels = level_cost.shape[0]
    selected = (
        pair_level[:, :, None] == jnp.arange(num_levels, dtype=jnp.int32)[None, None, :]
    ).astype(jnp.float32)
    return jnp.sum(selected * level_cost[None, None, :], axis=2)


def label_costs(row_labels, class_ids, labels_y):
    col_hot = (class_ids[:, None] == labels_y[None, :]).astype(jnp.float32)
    return jnp.dot(
        row_labels, col_hot, precision=lax.Precision.HIGHEST, preferred_element_type=jnp.float32
    )


def shards(train_embed, valid_embed, train_labels, valid_labels, pair_level, level_cost):
    rows_x, labels_x = (
        lax.all_gather(train_embed, "col", axis=0, tiled=True),
        lax.all_gather(train_labels, "col", axis=0, tiled=True),
    )
    width_d = rows_x.shape[1]
    classes = pair_level.shape[0]
    class_table = class_costs(pair_level, level_cost)
    class_ids = jnp.arange(classes, dtype=jnp.int32)
    train_hot = (labels_x[:, None] == class_ids[None, :]).astype(jnp.float32)
    row_labels = jnp.dot(
        train_hot, class_table, precision=lax.Precision.HIGHEST, preferred_element_type=jnp.float32
    )
    train_sq = squared_norms(rows_x)
    cols_y, labels_y = (
        lax.all_gather(valid_embed, "row", axis=0, tiled=True),
        lax.all_gather(valid_labels, "row", axis=0, tiled=True),
    )
    valid_sq = squared_norms(cols_y)
    label_full = label_costs(row_labels, class_ids, labels_y)

    def cost_block(offset, block_cols):
        block_y = lax.dynamic_slice_in_dim(cols_y, offset, block_cols, 0)
        block_sq = lax.dynamic_slice_in_dim(valid_sq, offset, block_cols, 0)
        label_slice = lax.dynamic_slice_in_dim(label_full, offset, block_cols, 1)
        return (
            train_sq[:, None] + block_sq[None, :] - 2.0 * inner_products(rows_x, block_y)
        ) / width_d + label_slice

    row_count = rows_x.shape[0]
    col_count = labels_y.shape[0]
    block_cols = min(512, col_count)
    block_count = col_count // block_cols
    block_ids = jnp.arange(block_count, dtype=jnp.int32)

    def scores(block_index, row_pot, col_pot):
        offset = block_index * block_cols
        cost_tile = cost_block(offset, block_cols)
        block_pot = lax.dynamic_slice_in_dim(col_pot, offset, block_cols, 0)
        return (
            (block_pot[None, :] - cost_tile) / entropy_scale,
            (row_pot[:, None] - cost_tile) / entropy_scale,
        )

    row_pot = jnp.zeros((row_count,), jnp.float32)
    col_pot = jnp.zeros((col_count,), jnp.float32)
    full_rows = row_count * lax.axis_size("row")
    full_cols = col_count * lax.axis_size("col")
    for iteration in range(ITERS):

        def local_peaks(running, block_index, row_pot=row_pot, col_pot=col_pot):
            row_side, col_side = scores(block_index, row_pot, col_pot)
            return (jnp.maximum(running, jnp.max(row_side, axis=1)), jnp.max(col_side, axis=0))

        row_local, col_local = lax.scan(
            local_peaks, jnp.full((row_count,), -jnp.inf, jnp.float32), block_ids
        )
        row_high = lax.pmax(row_local, "col")
        col_high = lax.pmax(col_local.reshape(col_count), "row")

        def local_totals(
            running,
            block_index,
            row_pot=row_pot,
            col_pot=col_pot,
            row_high=row_high,
            col_high=col_high,
        ):
            row_side, col_side = scores(block_index, row_pot, col_pot)
            block_high = lax.dynamic_slice_in_dim(col_high, block_index * block_cols, block_cols, 0)
            return (
                running + jnp.sum(jnp.exp(row_side - row_high[:, None]), axis=1),
                jnp.sum(jnp.exp(col_side - block_high[None, :]), axis=0),
            )

        row_part, col_part = lax.scan(local_totals, jnp.zeros((row_count,), jnp.float32), block_ids)
        row_sum = lax.psum(row_part, "col")
        col_sum = lax.psum(col_part.reshape(col_count), "row")
        row_new = entropy_scale * math.log(full_cols) - entropy_scale * (
            row_high + jnp.log(row_sum)
        )
        col_new = entropy_scale * math.log(full_rows) - entropy_scale * (
            col_high + jnp.log(col_sum)
        )
        row_pot = 0.5 * (row_pot + row_new)
        col_pot = 0.5 * (col_pot + col_new)
    potential_sum = lax.psum(jnp.sum(row_pot), "row")
    return (row_pot * full_rows - potential_sum) / (full_rows - 1)


def solution(mesh):
    placed = (
        P(("row", "col"), None),
        P(("row", "col"), None),
        P(("row", "col")),
        P(("row", "col")),
        P(),
        P(),
    )
    return jax.shard_map(shards, mesh=mesh, in_specs=placed, out_specs=P("row"), check_vma=False)
```

profile of v0, /device:TPU:1, one launch (start us, length us, event | category | flops | bytes accessed | tf_op | source)
XLA Modules:
  0.0 894.9 jit_solution(5116224132933514768)
XLA Ops:
  10.3 17.5 %all-reduce = s32[512]{0:T(512)S(1)} all-reduce(s32[512]{0:T(512)S(1)} %dynamic-update-slice), channel_id=1, replica_groups=mesh['row'=16,'col'=32] {'col'}, use_global_device_ids=true, to_apply=%add | all-reduce | flops 512 | bytes 4096
  27.7 28.0 %all-gather = s32[16,1,128]{2,1,0:T(1,128)S(1)} all-gather(s32[1,1,128]{2,1,0:T(1,128)} %bitcast.194), channel_id=1, replica_groups=mesh['row'=16,'col'=32] {'row'}, dimensions={0}, use_global_device_ids=true | all-gather | bytes 8704 | tf_op jit(solution)/shard_map/all_gather | solution.py:53
  55.7 34.7 %all_gather.12 = bf16[512,256]{1,0:T(8,128)(2,1)S(1)} all-gather(bf16[16,256]{1,0:T(8,128)(2,1)} %param.22), channel_id=1, replica_groups=mesh['row'=16,'col'=32] {'col'}, dimensions={0}, use_global_device_ids=true | all-gather | bytes 270336 | tf_op jit(solution)/shard_map/all_gather | solution.py:39
  92.0 3.8 fusion.60
  97.4 13.7 %while.100 = (s32[]{:T(128)}, f32[512]{0:T(512)S(1)}, f32[4,512]{1,0:T(4,128)S(1)}, f32[512]{0:T(512)S(1)}, s32[4]{0:T(128)S(1)}, /*index=5*/f32[2048]{0:T(1024)...) while((s32[]{:T(128)}, f32[512]{0:T(512)S(1)}, ...), condition=%wide.region_6.7_spmd.clone, body=%wide.region_3.6_spmd.clone.sunk | while | flops 136577024 | bytes 1596617 | solution.py:91
  111.1 36.0 %pmax.50 = f32[2048]{0:T(1024)S(1)} all-reduce(f32[2048]{0:T(1024)S(1)} %bitcast.188), channel_id=1, replica_groups=mesh['row'=16,'col'=32] {'row'}, use_global_device_ids=true, to_apply=%region_8.9 | all-reduce | flops 2048 | bytes 16384 | tf_op jit(solution)/shard_map/pmax | solution.py:95
  147.1 58.1 %pmax.49 = f32[512]{0:T(512)S(1)} all-reduce(f32[512]{0:T(512)S(1)} %get-tuple-element.462), channel_id=1, replica_groups=mesh['row'=16,'col'=32] {'col'}, use_global_device_ids=true, to_apply=%region_7.8 | all-reduce | flops 512 | bytes 4096 | tf_op jit(solution)/shard_map/pmax | solution.py:94
  205.2 14.1 %while.101 = (s32[]{:T(128)}, f32[512]{0:T(512)S(1)}, f32[4,512]{1,0:T(4,128)S(1)}, f32[512]{0:T(512)S(1)}, s32[4]{0:T(128)S(1)}, /*index=5*/f32[2048]{0:T(1024)...) while((s32[]{:T(128)}, f32[512]{0:T(512)S(1)}, ...), condition=%wide.region_12.13_spmd.clone, body=%wide.region_9.12_spmd.clone.sunk | while | flops 137101312 | bytes 1604829 | solution.py:112
  219.3 56.1 %psum.56 = f32[512]{0:T(512)S(1)} all-reduce(f32[512]{0:T(512)S(1)} %get-tuple-element.464), channel_id=1, replica_groups=mesh['row'=16,'col'=32] {'col'}, use_global_device_ids=true, to_apply=%region_13.14 | all-reduce | flops 512 | bytes 4096 | tf_op jit(solution)/shard_map/psum | solution.py:113
  275.5 51.8 %psum.57 = f32[2048]{0:T(1024)S(1)} all-reduce(f32[2048]{0:T(1024)S(1)} %bitcast.189), channel_id=1, replica_groups=mesh['row'=16,'col'=32] {'row'}, use_global_device_ids=true, to_apply=%region_14.15 | all-reduce | flops 2048 | bytes 16384 | tf_op jit(solution)/shard_map/psum | solution.py:114
  327.3 13.7 %while.102 = (s32[]{:T(128)}, f32[512]{0:T(512)S(1)}, f32[4,512]{1,0:T(4,128)S(1)}, s32[4]{0:T(128)S(1)}, f32[2048]{0:T(1024)S(1)}, /*index=5*/f32[512]{0:T(512)...) while((s32[]{:T(128)}, f32[512]{0:T(512)S(1)}, ...), condition=%wide.region_18.19_spmd.clone, body=%wide.region_15.18_spmd.clone.sunk | while | flops 137101312 | bytes 1604829 | solution.py:91
  341.0 24.0 %pmax.52 = f32[2048]{0:T(1024)S(1)} all-reduce(f32[2048]{0:T(1024)S(1)} %bitcast.190), channel_id=1, replica_groups=mesh['row'=16,'col'=32] {'row'}, use_global_device_ids=true, to_apply=%region_20.21 | all-reduce | flops 2048 | bytes 16384 | tf_op jit(solution)/shard_map/pmax | solution.py:95
  365.1 57.4 %pmax.51 = f32[512]{0:T(512)S(1)} all-reduce(f32[512]{0:T(512)S(1)} %get-tuple-element.466), channel_id=1, replica_groups=mesh['row'=16,'col'=32] {'col'}, use_global_device_ids=true, to_apply=%region_19.20 | all-reduce | flops 512 | bytes 4096 | tf_op jit(solution)/shard_map/pmax | solution.py:94
  422.5 14.9 %while.103 = (s32[]{:T(128)}, f32[512]{0:T(512)S(1)}, f32[4,512]{1,0:T(4,128)S(1)}, s32[4]{0:T(128)S(1)}, f32[2048]{0:T(1024)S(1)}, /*index=5*/f32[512]{0:T(512)...) while((s32[]{:T(128)}, f32[512]{0:T(512)S(1)}, ...), condition=%wide.region_24.25_spmd.clone, body=%wide.region_21.24_spmd.clone.sunk | while | flops 137625600 | bytes 1613041 | solution.py:112
  424.0 2.2 exponential_reduce_fusion.10
  427.7 2.2 exponential_reduce_fusion.10
  435.2 2.2 exponential_reduce_fusion.10
  437.4 56.1 %psum.58 = f32[512]{0:T(512)S(1)} all-reduce(f32[512]{0:T(512)S(1)} %get-tuple-element.468), channel_id=1, replica_groups=mesh['row'=16,'col'=32] {'col'}, use_global_device_ids=true, to_apply=%region_25.26 | all-reduce | flops 512 | bytes 4096 | tf_op jit(solution)/shard_map/psum | solution.py:113
  493.6 51.8 %psum.59 = f32[2048]{0:T(1024)S(1)} all-reduce(f32[2048]{0:T(1024)S(1)} %bitcast.191), channel_id=1, replica_groups=mesh['row'=16,'col'=32] {'row'}, use_global_device_ids=true, to_apply=%region_26.27 | all-reduce | flops 2048 | bytes 16384 | tf_op jit(solution)/shard_map/psum | solution.py:114
  545.4 13.5 %while.104 = (s32[]{:T(128)}, f32[512]{0:T(512)S(1)}, f32[4,512]{1,0:T(4,128)S(1)}, s32[4]{0:T(128)S(1)}, f32[2048]{0:T(1024)S(1)}, /*index=5*/f32[512]{0:T(512)...) while((s32[]{:T(128)}, f32[512]{0:T(512)S(1)}, ...), condition=%wide.region_30.31_spmd.clone, body=%wide.region_27.30_spmd.clone.sunk | while | flops 137101312 | bytes 1604829 | solution.py:91
  558.8 24.1 %pmax.54 = f32[2048]{0:T(1024)S(1)} all-reduce(f32[2048]{0:T(1024)S(1)} %bitcast.192), channel_id=1, replica_groups=mesh['row'=16,'col'=32] {'row'}, use_global_device_ids=true, to_apply=%region_32.33 | all-reduce | flops 2048 | bytes 16384 | tf_op jit(solution)/shard_map/pmax | solution.py:95
  582.9 57.4 %pmax.53 = f32[512]{0:T(512)S(1)} all-reduce(f32[512]{0:T(512)S(1)} %get-tuple-element.470), channel_id=1, replica_groups=mesh['row'=16,'col'=32] {'col'}, use_global_device_ids=true, to_apply=%region_31.32 | all-reduce | flops 512 | bytes 4096 | tf_op jit(solution)/shard_map/pmax | solution.py:94
  640.3 15.5 %while.105 = (s32[]{:T(128)}, f32[512]{0:T(512)S(1)}, f32[4,512]{1,0:T(4,128)S(1)}, s32[4]{0:T(128)S(1)}, f32[2048]{0:T(1024)S(1)}, /*index=5*/f32[512]{0:T(512)...) while((s32[]{:T(128)}, f32[512]{0:T(512)S(1)}, ...), condition=%wide.region_36.37_spmd.clone, body=%wide.region_33.36_spmd.clone.sunk | while | flops 137625600 | bytes 1613041 | solution.py:112
  641.9 2.2 exponential_reduce_fusion.11
  645.8 2.2 exponential_reduce_fusion.11
  649.7 2.2 exponential_reduce_fusion.11
  655.8 38.2 %psum.61 = f32[2048]{0:T(1024)S(1)} all-reduce(f32[2048]{0:T(1024)S(1)} %bitcast.193), channel_id=1, replica_groups=mesh['row'=16,'col'=32] {'row'}, use_global_device_ids=true, to_apply=%region_38.39 | all-reduce | flops 2048 | bytes 16384 | tf_op jit(solution)/shard_map/psum | solution.py:114
  694.1 13.1 %while.106 = (s32[]{:T(128)}, f32[512]{0:T(512)S(1)}, s32[4]{0:T(128)S(1)}, f32[2048]{0:T(1024)S(1)}, f32[512]{0:T(512)S(1)}, /*index=5*/f32[2048]{0:T(1024)S(1)...) while((s32[]{:T(128)}, f32[512]{0:T(512)S(1)}, ...), condition=%wide.region_41.42_spmd.clone, body=%wide.region_39.41_spmd.clone.sunk | while | flops 136315392 | bytes 1596617 | solution.py:91
  707.3 55.7 %pmax.55 = f32[512]{0:T(512)S(1)} all-reduce(f32[512]{0:T(512)S(1)} %get-tuple-element.474), channel_id=1, replica_groups=mesh['row'=16,'col'=32] {'col'}, use_global_device_ids=true, to_apply=%region_42.43 | all-reduce | flops 512 | bytes 4096 | tf_op jit(solution)/shard_map/pmax | solution.py:94
  763.0 13.4 %while.107 = (s32[]{:T(128)}, f32[512]{0:T(512)S(1)}, s32[4]{0:T(128)S(1)}, f32[2048]{0:T(1024)S(1)}, f32[512]{0:T(512)S(1)}, /*index=5*/f32[2048]{0:T(1024)S(1)...) while((s32[]{:T(128)}, f32[512]{0:T(512)S(1)}, ...), condition=%wide.region_45.46_spmd.clone, body=%wide.region_43.45_spmd.clone.sunk | while | flops 136577536 | bytes 1598673 | solution.py:112
  776.4 57.7 %all-reduce.1 = (f32[512]{0:T(512)S(1)}, f32[512]{0:T(512)S(1)}) all-reduce(f32[512]{0:T(512)S(1)} %get-tuple-element.475, f32[512]{0:T(512)S(1)} %get-tuple-element.472), channel_id=1, replica_groups=mesh['row'=16,'col'=32] {'col'}, use_global_device_ids=true, to_apply=%region_46.47 | all-reduce | flops 1024 | bytes 8192 | tf_op jit(solution)/shard_map/psum | solution.py:113
  834.7 52.1 %psum.63 = f32[]{:T(128)} all-reduce(f32[]{:T(128)} %get-tuple-element.1210), channel_id=1, replica_groups=mesh['row'=16,'col'=32] {'row'}, use_global_device_ids=true, to_apply=%region_48.49 | all-reduce | flops 1 | bytes 8 | tf_op jit(solution)/shard_map/psum | solution.py:123
  (227 shorter events, 85.6 us)
Async XLA Ops:
  6.5 89.3 %all-gather.3.cloned.1.call-start = ((), (), s32[]{:S(2)}) async-start(), calls=%async_computation | async-start | bytes 1114112 | tf_op jit(solution)/shard_map/all_gather | solution.py:52
Sparse Core Ops, SparseCore 0:
  9.5 48.0 all-gather.2
where the time goes:
time: 897 us; the launch traced here: 895 us
  blocking collectives  757 us (84%)
  matrix products  68.1 us (8%)
  local copies, waits for them, and re-layouts  28.5 us (3%)
  loops' own time  21.2 us (2%)
  between operations  14.4 us (2%)
    pmax x4, blocking collectives, shards(): row_high = lax.pmax(row_local, 'col')  229 us
    psum x3, blocking collectives, shards(): row_sum = lax.psum(row_part, 'col')  170 us
    psum x3, blocking collectives, shards(): col_sum = lax.psum(col_part.reshape(col_count), 'row')  142 us
    pmax x3, blocking collectives, shards(): col_high = lax.pmax(col_local.reshape(col_count), 'row')  84.1 us
    dot_general x32, matrix products, inner_products(): lax.dot_general(left_rows, right_rows, (((1,), (1,)), ((), ())), preferre...  64 us
    psum x1, blocking collectives, shards(): potential_sum = lax.psum(jnp.sum(row_pot), 'row')  52.1 us
    all_gather x1, blocking collectives, shards(): lax.all_gather(train_embed, 'col', axis=0, tiled=True)  34.7 us
    all_gather x1, blocking collectives, shards(): lax.all_gather(valid_labels, 'row', axis=0, tiled=True)  28 us
  transfers between devices with their start and end apart: 1, of which 0 were waited for; matrix products, arithmetic and copies ran while one was open for 1% of the time, Pallas kernels for 0%

commit v1 on v0

--- a/solution.py
+++ b/solution.py
@@ -36,7 +36,9 @@
 
 def shards(train_embed, valid_embed, train_labels, valid_labels, pair_level, level_cost):
     rows_x, labels_x = (
-        lax.all_gather(train_embed, "col", axis=0, tiled=True),
+        jnp.concatenate(
+            lax.all_to_all(jnp.stack([train_embed] * lax.axis_size("col")), "col", 0, 0), axis=0
+        ),
         lax.all_gather(train_labels, "col", axis=0, tiled=True),
     )
     width_d = rows_x.shape[1]

time: 897 us -> 859 us (0.958)
  blocking collectives: 757 us -> 707 us
  starting transfers between devices: 0.01 us -> 10.5 us
    all_gather x1 -> x0, blocking collectives: 34.7 us -> none  [shards(): lax.all_gather(train_embed, 'col', axis=0, tiled=True)]
    pmax x3, blocking collectives: 84.1 us -> 71.7 us  [shards(): col_high = lax.pmax(col_local.reshape(col_count), 'row')]
    all_to_all x0 -> x1, starting transfers between devices: none -> 10.5 us  [shards(): lax.all_to_all(jnp.stack([train_embed] * lax.axis_size('col')), 'col', 0, 0)]
  transfers between devices with their start and end apart: 1 -> 2, of which waited for: 0 -> 0; matrix products, arithmetic and copies ran while one was open for 1% -> 1% of each run, Pallas kernels for 0% -> 0%
where the time goes in v1:
time: 859 us; the launch traced here: 857 us
  blocking collectives  707 us (82%)
  matrix products  68.1 us (8%)
  local copies, waits for them, and re-layouts  29.7 us (3%)
  loops' own time  21.4 us (2%)
  between operations  14.4 us (2%)
  starting transfers between devices  10.5 us (1%)
    pmax x4, blocking collectives, shards(): row_high = lax.pmax(row_local, 'col')  226 us
    psum x3, blocking collectives, shards(): row_sum = lax.psum(row_part, 'col')  171 us
    psum x3, blocking collectives, shards(): col_sum = lax.psum(col_part.reshape(col_count), 'row')  142 us
    pmax x3, blocking collectives, shards(): col_high = lax.pmax(col_local.reshape(col_count), 'row')  71.7 us
    dot_general x32, matrix products, inner_products(): lax.dot_general(left_rows, right_rows, (((1,), (1,)), ((), ())), preferre...  63.9 us
    psum x1, blocking collectives, shards(): potential_sum = lax.psum(jnp.sum(row_pot), 'row')  52.1 us
    all_gather x1, blocking collectives, shards(): lax.all_gather(valid_labels, 'row', axis=0, tiled=True)  27.9 us
    dynamic_slice x32, local copies, waits for them, and re-layouts, shards(): lax.scan(local_peaks, jnp.full((row_count,), -jnp.inf, jnp.float32), bloc...  19.6 us
  transfers between devices with their start and end apart: 2, of which 0 were waited for; matrix products, arithmetic and copies ran while one was open for 1% of the time, Pallas kernels for 0%

profile of v1, /device:TPU:1, one launch (start us, length us, event | category | flops | bytes accessed | tf_op | source)
XLA Modules:
  0.0 857.4 jit_solution(4624202382016101675)
XLA Ops:
  8.7 10.5 %all-to-all-start = ((bf16[32,16,256]{2,1,0:T(8,128)(2,1)}), bf16[32,16,256]{2,1,0:T(8,128)(2,1)S(1)}, u32[]{:S(2)}, u32[]{:S(2)}) async-start(bf16[32,16,256]{2,1,0:T(8,128)(2,1)} %stack.2), calls=%async_computation | async-start | bytes 524288 | tf_op jit(solution)/shard_map/all_to_all | solution.py:40
  22.2 16.6 %all-reduce = s32[512]{0:T(512)S(1)} all-reduce(s32[512]{0:T(512)S(1)} %dynamic-update-slice), channel_id=1, replica_groups=mesh['row'=16,'col'=32] {'col'}, use_global_device_ids=true, to_apply=%add | all-reduce | flops 512 | bytes 4096
  38.7 27.9 %all-gather = s32[16,1,128]{2,1,0:T(1,128)S(1)} all-gather(s32[1,1,128]{2,1,0:T(1,128)} %bitcast.196), channel_id=1, replica_groups=mesh['row'=16,'col'=32] {'row'}, dimensions={0}, use_global_device_ids=true | all-gather | bytes 8704 | tf_op jit(solution)/shard_map/all_gather | solution.py:55
  68.1 3.8 fusion.60
  73.7 13.2 %while.100 = (s32[]{:T(128)}, f32[512]{0:T(512)S(1)}, f32[4,512]{1,0:T(4,128)S(1)}, f32[512]{0:T(512)S(1)}, s32[4]{0:T(128)S(1)}, /*index=5*/f32[2048]{0:T(1024)...) while((s32[]{:T(128)}, f32[512]{0:T(512)S(1)}, ...), condition=%wide.region_6.7_spmd.clone, body=%wide.region_3.6_spmd.clone.sunk | while | flops 136577024 | bytes 1596617 | solution.py:93
  87.0 23.6 %pmax.50 = f32[2048]{0:T(1024)S(1)} all-reduce(f32[2048]{0:T(1024)S(1)} %bitcast.190), channel_id=1, replica_groups=mesh['row'=16,'col'=32] {'row'}, use_global_device_ids=true, to_apply=%region_8.9 | all-reduce | flops 2048 | bytes 16384 | tf_op jit(solution)/shard_map/pmax | solution.py:97
  110.6 56.7 %pmax.49 = f32[512]{0:T(512)S(1)} all-reduce(f32[512]{0:T(512)S(1)} %get-tuple-element.462), channel_id=1, replica_groups=mesh['row'=16,'col'=32] {'col'}, use_global_device_ids=true, to_apply=%region_7.8 | all-reduce | flops 512 | bytes 4096 | tf_op jit(solution)/shard_map/pmax | solution.py:96
  167.3 14.4 %while.101 = (s32[]{:T(128)}, f32[512]{0:T(512)S(1)}, f32[4,512]{1,0:T(4,128)S(1)}, f32[512]{0:T(512)S(1)}, s32[4]{0:T(128)S(1)}, /*index=5*/f32[2048]{0:T(1024)...) while((s32[]{:T(128)}, f32[512]{0:T(512)S(1)}, ...), condition=%wide.region_12.13_spmd.clone, body=%wide.region_9.12_spmd.clone.sunk | while | flops 137101312 | bytes 1604829 | solution.py:114
  181.7 57.1 %psum.56 = f32[512]{0:T(512)S(1)} all-reduce(f32[512]{0:T(512)S(1)} %get-tuple-element.464), channel_id=1, replica_groups=mesh['row'=16,'col'=32] {'col'}, use_global_device_ids=true, to_apply=%region_13.14 | all-reduce | flops 512 | bytes 4096 | tf_op jit(solution)/shard_map/psum | solution.py:115
  238.8 51.8 %psum.57 = f32[2048]{0:T(1024)S(1)} all-reduce(f32[2048]{0:T(1024)S(1)} %bitcast.191), channel_id=1, replica_groups=mesh['row'=16,'col'=32] {'row'}, use_global_device_ids=true, to_apply=%region_14.15 | all-reduce | flops 2048 | bytes 16384 | tf_op jit(solution)/shard_map/psum | solution.py:116
  290.7 13.8 %while.102 = (s32[]{:T(128)}, f32[512]{0:T(512)S(1)}, f32[4,512]{1,0:T(4,128)S(1)}, s32[4]{0:T(128)S(1)}, f32[2048]{0:T(1024)S(1)}, /*index=5*/f32[512]{0:T(512)...) while((s32[]{:T(128)}, f32[512]{0:T(512)S(1)}, ...), condition=%wide.region_18.19_spmd.clone, body=%wide.region_15.18_spmd.clone.sunk | while | flops 137101312 | bytes 1604829 | solution.py:93
  304.5 24.1 %pmax.52 = f32[2048]{0:T(1024)S(1)} all-reduce(f32[2048]{0:T(1024)S(1)} %bitcast.192), channel_id=1, replica_groups=mesh['row'=16,'col'=32] {'row'}, use_global_device_ids=true, to_apply=%region_20.21 | all-reduce | flops 2048 | bytes 16384 | tf_op jit(solution)/shard_map/pmax | solution.py:97
  328.6 56.5 %pmax.51 = f32[512]{0:T(512)S(1)} all-reduce(f32[512]{0:T(512)S(1)} %get-tuple-element.466), channel_id=1, replica_groups=mesh['row'=16,'col'=32] {'col'}, use_global_device_ids=true, to_apply=%region_19.20 | all-reduce | flops 512 | bytes 4096 | tf_op jit(solution)/shard_map/pmax | solution.py:96
  385.1 15.0 %while.103 = (s32[]{:T(128)}, f32[512]{0:T(512)S(1)}, f32[4,512]{1,0:T(4,128)S(1)}, s32[4]{0:T(128)S(1)}, f32[2048]{0:T(1024)S(1)}, /*index=5*/f32[512]{0:T(512)...) while((s32[]{:T(128)}, f32[512]{0:T(512)S(1)}, ...), condition=%wide.region_24.25_spmd.clone, body=%wide.region_21.24_spmd.clone.sunk | while | flops 137625600 | bytes 1613041 | solution.py:114
  386.6 2.2 exponential_reduce_fusion.10
  397.9 2.2 exponential_reduce_fusion.10
  400.1 57.0 %psum.58 = f32[512]{0:T(512)S(1)} all-reduce(f32[512]{0:T(512)S(1)} %get-tuple-element.468), channel_id=1, replica_groups=mesh['row'=16,'col'=32] {'col'}, use_global_device_ids=true, to_apply=%region_25.26 | all-reduce | flops 512 | bytes 4096 | tf_op jit(solution)/shard_map/psum | solution.py:115
  457.1 51.8 %psum.59 = f32[2048]{0:T(1024)S(1)} all-reduce(f32[2048]{0:T(1024)S(1)} %bitcast.193), channel_id=1, replica_groups=mesh['row'=16,'col'=32] {'row'}, use_global_device_ids=true, to_apply=%region_26.27 | all-reduce | flops 2048 | bytes 16384 | tf_op jit(solution)/shard_map/psum | solution.py:116
  509.0 13.9 %while.104 = (s32[]{:T(128)}, f32[512]{0:T(512)S(1)}, f32[4,512]{1,0:T(4,128)S(1)}, s32[4]{0:T(128)S(1)}, f32[2048]{0:T(1024)S(1)}, /*index=5*/f32[512]{0:T(512)...) while((s32[]{:T(128)}, f32[512]{0:T(512)S(1)}, ...), condition=%wide.region_30.31_spmd.clone, body=%wide.region_27.30_spmd.clone.sunk | while | flops 137101312 | bytes 1604829 | solution.py:93
  522.9 24.1 %pmax.54 = f32[2048]{0:T(1024)S(1)} all-reduce(f32[2048]{0:T(1024)S(1)} %bitcast.194), channel_id=1, replica_groups=mesh['row'=16,'col'=32] {'row'}, use_global_device_ids=true, to_apply=%region_32.33 | all-reduce | flops 2048 | bytes 16384 | tf_op jit(solution)/shard_map/pmax | solution.py:97
  546.9 56.5 %pmax.53 = f32[512]{0:T(512)S(1)} all-reduce(f32[512]{0:T(512)S(1)} %get-tuple-element.470), channel_id=1, replica_groups=mesh['row'=16,'col'=32] {'col'}, use_global_device_ids=true, to_apply=%region_31.32 | all-reduce | flops 512 | bytes 4096 | tf_op jit(solution)/shard_map/pmax | solution.py:96
  603.4 15.0 %while.105 = (s32[]{:T(128)}, f32[512]{0:T(512)S(1)}, f32[4,512]{1,0:T(4,128)S(1)}, s32[4]{0:T(128)S(1)}, f32[2048]{0:T(1024)S(1)}, /*index=5*/f32[512]{0:T(512)...) while((s32[]{:T(128)}, f32[512]{0:T(512)S(1)}, ...), condition=%wide.region_36.37_spmd.clone, body=%wide.region_33.36_spmd.clone.sunk | while | flops 137625600 | bytes 1613041 | solution.py:114
  604.9 2.2 exponential_reduce_fusion.11
  608.7 2.2 exponential_reduce_fusion.11
  612.4 2.2 exponential_reduce_fusion.11
  616.2 2.2 exponential_reduce_fusion.11
  618.5 38.2 %psum.61 = f32[2048]{0:T(1024)S(1)} all-reduce(f32[2048]{0:T(1024)S(1)} %bitcast.195), channel_id=1, replica_groups=mesh['row'=16,'col'=32] {'row'}, use_global_device_ids=true, to_apply=%region_38.39 | all-reduce | flops 2048 | bytes 16384 | tf_op jit(solution)/shard_map/psum | solution.py:116
  656.8 13.0 %while.106 = (s32[]{:T(128)}, f32[512]{0:T(512)S(1)}, s32[4]{0:T(128)S(1)}, f32[2048]{0:T(1024)S(1)}, f32[512]{0:T(512)S(1)}, /*index=5*/f32[2048]{0:T(1024)S(1)...) while((s32[]{:T(128)}, f32[512]{0:T(512)S(1)}, ...), condition=%wide.region_41.42_spmd.clone, body=%wide.region_39.41_spmd.clone.sunk | while | flops 136315392 | bytes 1596617 | solution.py:93
  669.7 56.4 %pmax.55 = f32[512]{0:T(512)S(1)} all-reduce(f32[512]{0:T(512)S(1)} %get-tuple-element.474), channel_id=1, replica_groups=mesh['row'=16,'col'=32] {'col'}, use_global_device_ids=true, to_apply=%region_42.43 | all-reduce | flops 512 | bytes 4096 | tf_op jit(solution)/shard_map/pmax | solution.py:96
  726.1 13.4 %while.107 = (s32[]{:T(128)}, f32[512]{0:T(512)S(1)}, s32[4]{0:T(128)S(1)}, f32[2048]{0:T(1024)S(1)}, f32[512]{0:T(512)S(1)}, /*index=5*/f32[2048]{0:T(1024)S(1)...) while((s32[]{:T(128)}, f32[512]{0:T(512)S(1)}, ...), condition=%wide.region_45.46_spmd.clone, body=%wide.region_43.45_spmd.clone.sunk | while | flops 136577536 | bytes 1598673 | solution.py:114
  739.5 57.0 %all-reduce.1 = (f32[512]{0:T(512)S(1)}, f32[512]{0:T(512)S(1)}) all-reduce(f32[512]{0:T(512)S(1)} %get-tuple-element.475, f32[512]{0:T(512)S(1)} %get-tuple-element.472), channel_id=1, replica_groups=mesh['row'=16,'col'=32] {'col'}, use_global_device_ids=true, to_apply=%region_46.47 | all-reduce | flops 1024 | bytes 8192 | tf_op jit(solution)/shard_map/psum | solution.py:115
  797.2 52.1 %psum.63 = f32[]{:T(128)} all-reduce(f32[]{:T(128)} %get-tuple-element.1297), channel_id=1, replica_groups=mesh['row'=16,'col'=32] {'row'}, use_global_device_ids=true, to_apply=%region_48.49 | all-reduce | flops 1 | bytes 8 | tf_op jit(solution)/shard_map/psum | solution.py:125
  (230 shorter events, 86.8 us)
Async XLA Ops:
  6.5 65.6 %all-gather.3.cloned.1.call-start = ((), (), s32[]{:S(2)}) async-start(), calls=%async_computation.1 | async-start | bytes 1114112 | tf_op jit(solution)/shard_map/all_gather | solution.py:54
  8.7 63.2 %all-to-all-start = ((bf16[32,16,256]{2,1,0:T(8,128)(2,1)}), bf16[32,16,256]{2,1,0:T(8,128)(2,1)S(1)}, u32[]{:S(2)}, u32[]{:S(2)}) async-start(bf16[32,16,256]{2,1,0:T(8,128)(2,1)} %stack.2), calls=%async_computation | async-start | bytes 524288 | tf_op jit(solution)/shard_map/all_to_all | solution.py:40
Sparse Core Ops, SparseCore 0:
  9.5 47.8 all-gather.2
